TPU v7x, 32 devices: a whole 2x2x4 slice. The times are simulated.
32 devices in a mesh: grp: 2 (over y), tm: 4 (over z), sub: 2 (over x), ch: 2 (over core).
Axes of the slice: x: 2, y: 2, z: 4, core: 2. Of those that a mesh axis runs over, the one named last changes fastest.
Arguments:
- archive: float32 [16, 16384], P('ch', ('grp', 'tm')), parts along dimension 1, may hold values from -6 to 6
- tail: float32 [16, 254], P(None, 'grp'), parts along dimension 1, may hold values from -6 to 6
- precision: float32 [16, 16], replicated, may hold values from -1.5 to 1.5
- tile_list: int32 [8, 2, 2, 2], P(('grp', 'tm'), 'sub'), parts along dimension 0, may hold values from 0 to 15, as said below
Outputs:
- profile: float32 [16384], P(('grp', 'tm', 'sub')), parts along dimension 0
There are 2 independent parts, one for each index of `grp`. A program takes and returns all parts, laid end to end along the dimension named above; an argument that names none is the same for every part. Nothing has to cross between parts.
Inputs may be any that keep to these rules, and one draw needn't show every extreme that they name: `tile_list`: each pair has row block <= column block; every block k < 16 appears in some pair; pairs may repeat.
All inputs are finite; a program needn't handle non-finite values.
Results may differ from a plain program's by a relative error of at most 0.0003.
Values may be sent and summed in bfloat16 or wider, within the bound.
A program may use at most 128 MiB of HBM per device.

v0:
```python
import functools

import jax
import jax.numpy as jnp
from jax import lax
from jax.experimental import pallas as pl
from jax.experimental.pallas import tpu as pltpu
from jax.sharding import PartitionSpec as P

M = 128
TS = 512
SLOTS = 2
DEPTH = 2048
EXCL = 32
LANES = 128
STEP = 16
COLS = TS + M
ROWS = TS // 2 + M
SPAN = COLS + ROWS
MESH = pl.DeviceIdType.MESH


def whiten(factor, samples):
    return jnp.dot(
        factor, samples, precision=lax.Precision.HIGHEST, preferred_element_type=jnp.float32
    ).astype(jnp.bfloat16)


def kernel(
    n_tm,
    n_sub,
    tiles_ref,
    archive_ref,
    tail_ref,
    precision_ref,
    out_ref,
    raw_ref,
    series_ref,
    hankel_ref,
    lagged_ref,
    mine_ref,
    theirs_ref,
    raw_sems,
    time_send,
    time_recv,
    pair_send,
    pair_recv,
    min_sems,
):
    tm, sub, ch = lax.axis_index("tm"), lax.axis_index("sub"), lax.axis_index("ch")
    other = 1 - ch
    group = n_tm * n_sub * 2
    me = (tm * n_sub + sub) * 2 + ch
    channels, span = archive_ref.shape
    half = span // 2
    starts_all = n_tm * span

    def place(rank):
        owner = rank // 2
        return {"tm": owner // n_sub, "sub": owner % n_sub, "ch": rank % 2}

    def each_peer(action):
        if group <= 16:
            for step in range(1, group):
                action(step)
        else:
            lax.fori_loop(1, group, lambda step, _: (action(step), 0)[1], 0)

    barrier = pltpu.get_barrier_semaphore()
    each_peer(
        lambda step: pl.semaphore_signal(
            barrier, inc=1, device_id=place(lax.rem(me + step, group)), device_id_type=MESH
        )
    )
    own_rows = pl.ds(pl.multiple_of(ch * channels, channels), channels)
    raw_ref[own_rows, :] = archive_ref[:, pl.ds(pl.multiple_of(ch * half, half), half)]
    factor = precision_ref[...]
    last = starts_all // LANES
    series_ref[last] = jnp.zeros((2 * channels, LANES), jnp.bfloat16)
    series_ref[last, :, : M - 1] = whiten(factor, tail_ref[...])
    pl.semaphore_wait(barrier, group - 1)

    swap = pltpu.make_async_remote_copy(
        src_ref=archive_ref.at[:, pl.ds(pl.multiple_of(other * half, half), half)],
        dst_ref=raw_ref.at[own_rows, :],
        send_sem=raw_sems.at[0],
        recv_sem=raw_sems.at[1],
        device_id={"ch": other},
        device_id_type=MESH,
    )
    swap.start()
    swap.wait_recv()

    tiles = half // LANES

    def chunk(owner, part):
        return series_ref.at[pl.ds((owner * 2 + part) * tiles, tiles)]

    mine = chunk(tm, ch)
    whitened = whiten(factor, raw_ref[...])
    for k in range(tiles):
        series_ref[(tm * 2 + ch) * tiles + k] = whitened[:, k * LANES : (k + 1) * LANES]
    along_time = [None]
    for back in range(1, n_tm):
        along_time.append(
            pltpu.make_async_remote_copy(
                src_ref=mine,
                dst_ref=mine,
                send_sem=time_send.at[back],
                recv_sem=time_recv.at[back],
                device_id={"tm": lax.rem(tm + back, n_tm)},
                device_id_type=MESH,
            )
        )
        along_time[back].start()
    to_pair = []
    for back in range(n_tm):
        if back:
            along_time[back].wait_recv()
        held = chunk(lax.rem(tm + n_tm - back, n_tm), ch)
        to_pair.append(
            pltpu.make_async_remote_copy(
                src_ref=held,
                dst_ref=held,
                send_sem=pair_send.at[back],
                recv_sem=pair_recv.at[back],
                device_id={"ch": other},
                device_id_type=MESH,
            )
        )
        to_pair[back].start()
    for copy in to_pair:
        copy.wait_recv()

    pieces = []
    for slot in range(SLOTS):
        per_block = TS // LANES
        row_tile = tiles_ref[0, 0, slot, 0] * per_block + ch * (per_block // 2)
        col_tile = tiles_ref[0, 0, slot, 1] * per_block
        pieces.extend(series_ref[col_tile + k] for k in range(COLS // LANES))
        pieces.extend(series_ref[row_tile + k] for k in range(ROWS // LANES))
    segment = jnp.concatenate(pieces, axis=1).astype(jnp.float32)
    width = segment.shape[1]
    depth = segment.shape[0]
    for lag in range(STEP):
        moved = segment if lag == 0 else pltpu.roll(segment, width - lag, axis=1)
        hankel_ref[lag * depth : (lag + 1) * depth, :] = moved.astype(jnp.bfloat16)
    size = STEP * depth
    unit = (
        lax.broadcasted_iota(jnp.int32, (size, size), 0)
        == lax.broadcasted_iota(jnp.int32, (size, size), 1)
    ).astype(jnp.bfloat16)
    for at in range(0, width, size):
        lagged_ref[at : at + size, :] = lax.dot_general(
            unit,
            hankel_ref[:, at : at + size],
            (((1,), (1,)), ((), ())),
            preferred_element_type=jnp.float32,
        ).astype(jnp.bfloat16)
    norms = jnp.broadcast_to(jnp.sum(segment * segment, axis=0, keepdims=True), (8, width))
    shift = 1
    while shift < M:
        norms = norms + pltpu.roll(norms, width - shift, axis=1)
        shift *= 2

    owners, piece_rows, _ = mine_ref.shape
    place_shape = (owners, piece_rows, LANES)
    line = lax.broadcasted_iota(jnp.int32, place_shape, 0) * piece_rows
    line = line + lax.broadcasted_iota(jnp.int32, place_shape, 1)
    block_of, part_of = line // per_block, line % per_block
    best = jnp.full(place_shape, jnp.inf, jnp.float32)
    for slot in range(SLOTS):
        col_at = slot * SPAN
        row_at = col_at + COLS
        n_rows = TS // 2
        left = jnp.concatenate(
            [lagged_ref[row_at + v : row_at + v + n_rows, :] for v in range(0, M, STEP)], axis=1
        )
        right = jnp.concatenate(
            [lagged_ref[col_at + v : col_at + v + TS, :] for v in range(0, M, STEP)], axis=1
        )
        products = lax.dot_general(
            left, right, (((1,), (1,)), ((), ())), preferred_element_type=jnp.float32
        )
        row_block = tiles_ref[0, 0, slot, 0]
        col_block = tiles_ref[0, 0, slot, 1]
        between = row_block * TS + ch * n_rows - col_block * TS
        separation = (
            lax.broadcasted_iota(jnp.int32, (n_rows, TS), 0)
            - lax.broadcasted_iota(jnp.int32, (n_rows, TS), 1)
            + between
        )
        scores = jnp.where(jnp.abs(separation) < EXCL, jnp.inf, -2.0 * products)
        row_norms = norms[:1, row_at : row_at + n_rows]
        col_norms = norms[:1, col_at : col_at + TS]
        row_wide = jnp.transpose(jnp.broadcast_to(row_norms, (LANES, n_rows)))
        by_col = jnp.min(scores + jnp.concatenate([row_wide] * per_block, axis=1), axis=0, keepdims=True)
        by_col = (by_col + col_norms) * (1.0 / DEPTH)
        with_col = scores + col_norms
        folded = with_col[:, :LANES]
        for q in range(1, per_block):
            folded = jnp.minimum(folded, with_col[:, q * LANES : (q + 1) * LANES])
        by_row = jnp.min(jnp.transpose(folded), axis=0, keepdims=True)
        by_row = (by_row + row_norms) * (1.0 / DEPTH)
        for q in range(per_block):
            here = by_col[:, q * LANES : (q + 1) * LANES].reshape(1, 1, LANES)
            hit = (block_of == col_block) & (part_of == q)
            best = jnp.minimum(best, jnp.where(hit, here, jnp.inf))
        for q in range(per_block // 2):
            here = by_row[:, q * LANES : (q + 1) * LANES].reshape(1, 1, LANES)
            hit = (block_of == row_block) & (part_of == q + ch * (per_block // 2))
            best = jnp.minimum(best, jnp.where(hit, here, jnp.inf))
    mine_ref[...] = best

    def send_minima(step):
        rank = lax.rem(me + step, group)
        pltpu.make_async_remote_copy(
            src_ref=mine_ref.at[rank // 2],
            dst_ref=theirs_ref.at[step - 1],
            send_sem=min_sems.at[0],
            recv_sem=min_sems.at[1],
            device_id=place(rank),
            device_id_type=MESH,
        ).start()

    each_peer(send_minima)
    every = pltpu.make_async_remote_copy(
        src_ref=theirs_ref,
        dst_ref=theirs_ref,
        send_sem=min_sems.at[0],
        recv_sem=min_sems.at[1],
        device_id={"ch": other},
        device_id_type=MESH,
    )
    every.wait_recv()
    out_ref[...] = jnp.minimum(mine_ref[me // 2], jnp.min(theirs_ref[...], axis=0))
    every.wait_send()
    swap.wait_send()
    for copy in along_time[1:] + to_pair:
        copy.wait_send()


def body(archive, tail, precision, tile_list):
    n_tm, n_sub = lax.axis_size("tm"), lax.axis_size("sub")
    group = n_tm * n_sub * 2
    channels, span = archive.shape
    starts_all = span * n_tm
    piece_rows = starts_all // (n_tm * n_sub) // LANES
    every = 2 * channels
    width = SLOTS * SPAN
    vmem = pl.BlockSpec(memory_space=pltpu.VMEM)
    out = pl.pallas_call(
        functools.partial(kernel, n_tm, n_sub),
        out_shape=jax.ShapeDtypeStruct((piece_rows, LANES), jnp.float32),
        in_specs=[pl.BlockSpec(memory_space=pltpu.SMEM), vmem, vmem, vmem],
        out_specs=vmem,
        scratch_shapes=[
            pltpu.VMEM((every, span // 2), jnp.float32),
            pltpu.VMEM((starts_all // LANES + 1, every, LANES), jnp.bfloat16),
            pltpu.VMEM((STEP * every, width), jnp.bfloat16),
            pltpu.VMEM((width, STEP * every), jnp.bfloat16),
            pltpu.VMEM((n_tm * n_sub, piece_rows, LANES), jnp.float32),
            pltpu.VMEM((group - 1, piece_rows, LANES), jnp.float32),
            pltpu.SemaphoreType.DMA((2,)),
            pltpu.SemaphoreType.DMA((n_tm,)),
            pltpu.SemaphoreType.DMA((n_tm,)),
            pltpu.SemaphoreType.DMA((n_tm,)),
            pltpu.SemaphoreType.DMA((n_tm,)),
            pltpu.SemaphoreType.DMA((2,)),
        ],
        compiler_params=pltpu.CompilerParams(
            collective_id=0, has_side_effects=True, vmem_limit_bytes=40 * 2**20
        ),
    )(tile_list, archive, tail, precision)
    return out.reshape(-1)


def solution(mesh):
    placed = (P("ch", ("grp", "tm")), P(None, "grp"), P(), P(("grp", "tm"), "sub", None, None))
    return jax.shard_map(
        body, mesh=mesh, in_specs=placed, out_specs=P(("grp", "tm", "sub")), check_vma=False
    )
```

profile of v0, /device:TPU:0, one launch (start us, length us, event | category | flops | bytes accessed | tf_op | source)
XLA Modules:
  0.0 22.6 jit_solution(16429414141448880450)
XLA Ops:
  0.0 0.0 copy-start
  0.0 0.8 %copy-done = f32[8,2048]{1,0:T(8,128)S(1)} copy-done((f32[8,2048]{1,0:T(8,128)S(1)}, f32[8,2048]{1,0:T(8,128)}, u32[]{:S(2)}) %copy-start) | copy-done | bytes 65560
  0.8 0.0 copy-start.1
  0.8 0.7 %copy-done.1 = f32[16,127]{1,0:T(8,128)S(1)} copy-done((f32[16,127]{1,0:T(8,128)S(1)}, f32[16,127]{1,0:T(8,128)}, u32[]{:S(2)}) %copy-start.1) | copy-done | bytes 8152
  1.5 0.0 copy-start.2
  1.5 0.7 %copy-done.2 = f32[16,16]{1,0:T(8,128)S(1)} copy-done((f32[16,16]{1,0:T(8,128)S(1)}, f32[16,16]{1,0:T(8,128)}, u32[]{:S(2)}) %copy-start.2) | copy-done | bytes 1048
  2.2 0.0 copy-start.3
  2.2 0.7 %copy-done.3 = s32[1,1,2,2]{3,2,1,0:T(2,128)S(1)} copy-done((s32[1,1,2,2]{3,2,1,0:T(2,128)S(1)}, s32[1,1,2,2]{3,2,1,0:T(2,128)}, u32[]{:S(2)}) %copy-start.3) | copy-done | bytes 40
  2.9 19.0 %shard_map.46 = f32[8,128]{1,0:T(8,128)S(1)} custom-call(s32[1,1,2,2]{3,2,1,0:T(2,128)S(1)} %copy-done.3, f32[8,2048]{1,0:T(8,128)S(1)} %copy-done, f32[16,127]{1,0:T(8,128)S(1)} %copy-done.1, f32[16,16]{1,0:T(8,128)S(1)} %copy-done.2), custom_call_target="tpu_custom_call" | custom-call | tf_op jit(solution)/shard_map/pallas_call | solution.py:252
  22.0 0.6 %copy.6 = f32[1024]{0:T(1024)} copy(f32[1024]{0:T(1024)S(1)} %bitcast.1) | data formatting | bytes 8192
Async XLA Ops:
  0.0 0.8 %copy-start = (f32[8,2048]{1,0:T(8,128)S(1)}, f32[8,2048]{1,0:T(8,128)}, u32[]{:S(2)}) copy-start(f32[8,2048]{1,0:T(8,128)} %archive_ref.1) | copy-start | bytes 196612
  0.8 0.7 %copy-start.1 = (f32[16,127]{1,0:T(8,128)S(1)}, f32[16,127]{1,0:T(8,128)}, u32[]{:S(2)}) copy-start(f32[16,127]{1,0:T(8,128)} %tail_ref.1) | copy-start | bytes 24388
  1.5 0.7 %copy-start.2 = (f32[16,16]{1,0:T(8,128)S(1)}, f32[16,16]{1,0:T(8,128)}, u32[]{:S(2)}) copy-start(f32[16,16]{1,0:T(8,128)} %precision_ref.1) | copy-start | bytes 3076
  2.2 0.7 %copy-start.3 = (s32[1,1,2,2]{3,2,1,0:T(2,128)S(1)}, s32[1,1,2,2]{3,2,1,0:T(2,128)}, u32[]{:S(2)}) copy-start(s32[1,1,2,2]{3,2,1,0:T(2,128)} %tiles_ref.1) | copy-start | bytes 52
where the time goes:
time: 22.8 us; the launch traced here: 22.6 us
  Pallas kernels  19 us (83%)
  local copies, waits for them, and re-layouts  3.51 us (15%)
    pallas_call x1, Pallas kernels, body(): pl.pallas_call(functools.partial(kernel, n_tm, n_sub), out_shape=jax.Shap...  19 us
    unnamed x9, local copies, waits for them, and re-layouts  3.51 us

commit v1 on v0

--- a/solution.py
+++ b/solution.py
@@ -29,17 +29,21 @@
 def kernel(
     n_tm,
     n_sub,
+    tiles_hbm,
+    archive_ref,
+    tail_hbm,
+    precision_hbm,
+    out_ref,
     tiles_ref,
-    archive_ref,
     tail_ref,
     precision_ref,
-    out_ref,
     raw_ref,
     series_ref,
     hankel_ref,
     lagged_ref,
     mine_ref,
     theirs_ref,
+    load_sems,
     raw_sems,
     time_send,
     time_recv,
@@ -66,14 +70,29 @@
         else:
             lax.fori_loop(1, group, lambda step, _: (action(step), 0)[1], 0)
 
+    own_rows = pl.ds(pl.multiple_of(ch * channels, channels), channels)
+    own_half = archive_ref.at[:, pl.ds(pl.multiple_of(ch * half, half), half)]
+    loads = [
+        pltpu.make_async_copy(source, target, load_sems.at[at])
+        for at, (source, target) in enumerate(
+            (
+                (precision_hbm, precision_ref),
+                (tail_hbm, tail_ref),
+                (own_half, raw_ref.at[own_rows, :]),
+                (tiles_hbm, tiles_ref),
+            )
+        )
+    ]
+    for load in loads:
+        load.start()
     barrier = pltpu.get_barrier_semaphore()
     each_peer(
         lambda step: pl.semaphore_signal(
             barrier, inc=1, device_id=place(lax.rem(me + step, group)), device_id_type=MESH
         )
     )
-    own_rows = pl.ds(pl.multiple_of(ch * channels, channels), channels)
-    raw_ref[own_rows, :] = archive_ref[:, pl.ds(pl.multiple_of(ch * half, half), half)]
+    for load in loads[:2]:
+        load.wait()
     factor = precision_ref[...]
     last = starts_all // LANES
     series_ref[last] = jnp.zeros((2 * channels, LANES), jnp.bfloat16)
@@ -89,6 +108,8 @@
         device_id_type=MESH,
     )
     swap.start()
+    for load in loads[2:]:
+        load.wait()
     swap.wait_recv()
 
     tiles = half // LANES
@@ -248,19 +269,23 @@
     piece_rows = starts_all // (n_tm * n_sub) // LANES
     every = 2 * channels
     width = SLOTS * SPAN
-    vmem = pl.BlockSpec(memory_space=pltpu.VMEM)
+    anywhere = pl.BlockSpec(memory_space=pl.ANY)
     out = pl.pallas_call(
         functools.partial(kernel, n_tm, n_sub),
         out_shape=jax.ShapeDtypeStruct((piece_rows, LANES), jnp.float32),
-        in_specs=[pl.BlockSpec(memory_space=pltpu.SMEM), vmem, vmem, vmem],
-        out_specs=vmem,
+        in_specs=[anywhere] * 4,
+        out_specs=pl.BlockSpec(memory_space=pltpu.VMEM),
         scratch_shapes=[
+            pltpu.SMEM(tile_list.shape, jnp.int32),
+            pltpu.VMEM(tail.shape, jnp.float32),
+            pltpu.VMEM(precision.shape, jnp.float32),
             pltpu.VMEM((every, span // 2), jnp.float32),
             pltpu.VMEM((starts_all // LANES + 1, every, LANES), jnp.bfloat16),
             pltpu.VMEM((STEP * every, width), jnp.bfloat16),
             pltpu.VMEM((width, STEP * every), jnp.bfloat16),
             pltpu.VMEM((n_tm * n_sub, piece_rows, LANES), jnp.float32),
             pltpu.VMEM((group - 1, piece_rows, LANES), jnp.float32),
+            pltpu.SemaphoreType.DMA((4,)),
             pltpu.SemaphoreType.DMA((2,)),
             pltpu.SemaphoreType.DMA((n_tm,)),
             pltpu.SemaphoreType.DMA((n_tm,)),
@@ -269,7 +294,7 @@
             pltpu.SemaphoreType.DMA((2,)),
         ],
         compiler_params=pltpu.CompilerParams(
-            collective_id=0, has_side_effects=True, vmem_limit_bytes=40 * 2**20
+            collective_id=0, has_side_effects=True, vmem_limit_bytes=60 * 2**20
         ),
     )(tile_list, archive, tail, precision)
     return out.reshape(-1)

time: 22.8 us -> 20.7 us (0.908)
  local copies, waits for them, and re-layouts: 3.51 us -> 1.28 us
    unnamed x9 -> x1, local copies, waits for them, and re-layouts: 3.51 us -> 1.28 us
where the time goes in v1:
time: 20.7 us; the launch traced here: 20.5 us
  Pallas kernels  19.2 us (93%)
  local copies, waits for them, and re-layouts  1.28 us (6%)
    pallas_call x1, Pallas kernels, body(): pl.pallas_call(functools.partial(kernel, n_tm, n_sub), out_shape=jax.Shap...  19.2 us
    unnamed x1, local copies, waits for them, and re-layouts  1.28 us

profile of v1, /device:TPU:0, one launch (start us, length us, event | category | flops | bytes accessed | tf_op | source)
XLA Modules:
  0.0 20.5 jit_solution(18330265550520952418)
XLA Ops:
  0.0 19.2 %shard_map.46 = f32[8,128]{1,0:T(8,128)} custom-call(s32[1,1,2,2]{3,2,1,0:T(2,128)} %tiles_hbm.1, f32[8,2048]{1,0:T(8,128)} %archive_ref.1, f32[16,127]{1,0:T(8,128)} %tail_hbm.1, f32[16,16]{1,0:T(8,128)} %precision_hbm.1), custom_call_target="tpu_custom_call" | custom-call | tf_op jit(solution)/shard_map/pallas_call | solution.py:273
  19.2 1.3 %copy.6 = f32[1024]{0:T(1024)} copy(f32[1024]{0:T(1024)} %bitcast.1) | data formatting | bytes 8192

commit v2 on v1

--- a/solution.py
+++ b/solution.py
@@ -59,16 +59,23 @@
     half = span // 2
     starts_all = n_tm * span
 
+    def crossed(a, b, count):
+        total, bit = 0, 1
+        while bit < count:
+            total = total + lax.rem(a // bit + b // bit, 2) * bit
+            bit *= 2
+        return total
+
     def place(rank):
         owner = rank // 2
         return {"tm": owner // n_sub, "sub": owner % n_sub, "ch": rank % 2}
 
     def each_peer(action):
         if group <= 16:
-            for step in range(1, group):
+            for step in reversed(range(1, group)):
                 action(step)
         else:
-            lax.fori_loop(1, group, lambda step, _: (action(step), 0)[1], 0)
+            lax.fori_loop(1, group, lambda step, _: (action(group - step), 0)[1], 0)
 
     own_rows = pl.ds(pl.multiple_of(ch * channels, channels), channels)
     own_half = archive_ref.at[:, pl.ds(pl.multiple_of(ch * half, half), half)]
@@ -88,7 +95,7 @@
     barrier = pltpu.get_barrier_semaphore()
     each_peer(
         lambda step: pl.semaphore_signal(
-            barrier, inc=1, device_id=place(lax.rem(me + step, group)), device_id_type=MESH
+            barrier, inc=1, device_id=place(crossed(me, step, group)), device_id_type=MESH
         )
     )
     for load in loads[:2]:
@@ -121,35 +128,33 @@
     whitened = whiten(factor, raw_ref[...])
     for k in range(tiles):
         series_ref[(tm * 2 + ch) * tiles + k] = whitened[:, k * LANES : (k + 1) * LANES]
-    along_time = [None]
-    for back in range(1, n_tm):
-        along_time.append(
-            pltpu.make_async_remote_copy(
-                src_ref=mine,
-                dst_ref=mine,
-                send_sem=time_send.at[back],
-                recv_sem=time_recv.at[back],
-                device_id={"tm": lax.rem(tm + back, n_tm)},
-                device_id_type=MESH,
-            )
-        )
-        along_time[back].start()
+    along_time = [None] * n_tm
+    for far in sorted(range(1, n_tm), key=lambda d: (d < n_tm // 2, d)):
+        along_time[far] = pltpu.make_async_remote_copy(
+            src_ref=mine,
+            dst_ref=mine,
+            send_sem=time_send.at[far],
+            recv_sem=time_recv.at[far],
+            device_id={"tm": crossed(tm, far, n_tm)},
+            device_id_type=MESH,
+        )
+        along_time[far].start()
     to_pair = []
-    for back in range(n_tm):
-        if back:
-            along_time[back].wait_recv()
-        held = chunk(lax.rem(tm + n_tm - back, n_tm), ch)
+    for far in range(n_tm):
+        if far:
+            along_time[far].wait_recv()
+        held = chunk(crossed(tm, far, n_tm), ch)
         to_pair.append(
             pltpu.make_async_remote_copy(
                 src_ref=held,
                 dst_ref=held,
-                send_sem=pair_send.at[back],
-                recv_sem=pair_recv.at[back],
+                send_sem=pair_send.at[far],
+                recv_sem=pair_recv.at[far],
                 device_id={"ch": other},
                 device_id_type=MESH,
             )
         )
-        to_pair[back].start()
+        to_pair[far].start()
     for copy in to_pair:
         copy.wait_recv()
 
@@ -234,7 +239,7 @@
     mine_ref[...] = best
 
     def send_minima(step):
-        rank = lax.rem(me + step, group)
+        rank = crossed(me, step, group)
         pltpu.make_async_remote_copy(
             src_ref=mine_ref.at[rank // 2],
             dst_ref=theirs_ref.at[step - 1],

time: 20.7 us -> 20.8 us (level)
  no operation moved by 1% of the time
where the time goes in v2:
time: 20.8 us; the launch traced here: 20.6 us
  Pallas kernels  19.3 us (93%)
  local copies, waits for them, and re-layouts  1.28 us (6%)
    pallas_call x1, Pallas kernels, body(): pl.pallas_call(functools.partial(kernel, n_tm, n_sub), out_shape=jax.Shap...  19.3 us
    unnamed x1, local copies, waits for them, and re-layouts  1.28 us

profile of v2, /device:TPU:0, one launch (start us, length us, event | category | flops | bytes accessed | tf_op | source)
XLA Modules:
  0.0 20.6 jit_solution(12169343707761161013)
XLA Ops:
  0.0 19.3 %shard_map.46 = f32[8,128]{1,0:T(8,128)} custom-call(s32[1,1,2,2]{3,2,1,0:T(2,128)} %tiles_hbm.1, f32[8,2048]{1,0:T(8,128)} %archive_ref.1, f32[16,127]{1,0:T(8,128)} %tail_hbm.1, f32[16,16]{1,0:T(8,128)} %precision_hbm.1), custom_call_target="tpu_custom_call" | custom-call | tf_op jit(solution)/shard_map/pallas_call | solution.py:278
  19.3 1.3 %copy.6 = f32[1024]{0:T(1024)} copy(f32[1024]{0:T(1024)} %bitcast.1) | data formatting | bytes 8192

commit v3 on v2

--- a/solution.py
+++ b/solution.py
@@ -42,6 +42,8 @@
     hankel_ref,
     lagged_ref,
     mine_ref,
+    pair_ref,
+    merged_ref,
     theirs_ref,
     load_sems,
     raw_sems,
@@ -49,12 +51,13 @@
     time_recv,
     pair_send,
     pair_recv,
+    merge_sems,
     min_sems,
 ):
     tm, sub, ch = lax.axis_index("tm"), lax.axis_index("sub"), lax.axis_index("ch")
     other = 1 - ch
-    group = n_tm * n_sub * 2
-    me = (tm * n_sub + sub) * 2 + ch
+    group = n_tm * n_sub
+    me = tm * n_sub + sub
     channels, span = archive_ref.shape
     half = span // 2
     starts_all = n_tm * span
@@ -66,9 +69,8 @@
             bit *= 2
         return total
 
-    def place(rank):
-        owner = rank // 2
-        return {"tm": owner // n_sub, "sub": owner % n_sub, "ch": rank % 2}
+    def place(owner):
+        return {"tm": owner // n_sub, "sub": owner % n_sub}
 
     def each_peer(action):
         if group <= 16:
@@ -98,13 +100,14 @@
             barrier, inc=1, device_id=place(crossed(me, step, group)), device_id_type=MESH
         )
     )
+    pl.semaphore_signal(barrier, inc=1, device_id={"ch": other}, device_id_type=MESH)
     for load in loads[:2]:
         load.wait()
     factor = precision_ref[...]
     last = starts_all // LANES
     series_ref[last] = jnp.zeros((2 * channels, LANES), jnp.bfloat16)
     series_ref[last, :, : M - 1] = whiten(factor, tail_ref[...])
-    pl.semaphore_wait(barrier, group - 1)
+    pl.semaphore_wait(barrier, group)
 
     swap = pltpu.make_async_remote_copy(
         src_ref=archive_ref.at[:, pl.ds(pl.multiple_of(other * half, half), half)],
@@ -238,14 +241,26 @@
             best = jnp.minimum(best, jnp.where(hit, here, jnp.inf))
     mine_ref[...] = best
 
+    merge = pltpu.make_async_remote_copy(
+        src_ref=mine_ref,
+        dst_ref=pair_ref,
+        send_sem=merge_sems.at[0],
+        recv_sem=merge_sems.at[1],
+        device_id={"ch": other},
+        device_id_type=MESH,
+    )
+    merge.start()
+    merge.wait_recv()
+    merged_ref[...] = jnp.minimum(best, pair_ref[...])
+
     def send_minima(step):
-        rank = crossed(me, step, group)
+        owner = crossed(me, step, group)
         pltpu.make_async_remote_copy(
-            src_ref=mine_ref.at[rank // 2],
+            src_ref=merged_ref.at[owner],
             dst_ref=theirs_ref.at[step - 1],
             send_sem=min_sems.at[0],
             recv_sem=min_sems.at[1],
-            device_id=place(rank),
+            device_id=place(owner),
             device_id_type=MESH,
         ).start()
 
@@ -259,7 +274,8 @@
         device_id_type=MESH,
     )
     every.wait_recv()
-    out_ref[...] = jnp.minimum(mine_ref[me // 2], jnp.min(theirs_ref[...], axis=0))
+    out_ref[...] = jnp.minimum(merged_ref[me], jnp.min(theirs_ref[...], axis=0))
+    merge.wait_send()
     every.wait_send()
     swap.wait_send()
     for copy in along_time[1:] + to_pair:
@@ -268,7 +284,7 @@
 
 def body(archive, tail, precision, tile_list):
     n_tm, n_sub = lax.axis_size("tm"), lax.axis_size("sub")
-    group = n_tm * n_sub * 2
+    group = n_tm * n_sub
     channels, span = archive.shape
     starts_all = span * n_tm
     piece_rows = starts_all // (n_tm * n_sub) // LANES
@@ -288,7 +304,9 @@
             pltpu.VMEM((starts_all // LANES + 1, every, LANES), jnp.bfloat16),
             pltpu.VMEM((STEP * every, width), jnp.bfloat16),
             pltpu.VMEM((width, STEP * every), jnp.bfloat16),
-            pltpu.VMEM((n_tm * n_sub, piece_rows, LANES), jnp.float32),
+            pltpu.VMEM((group, piece_rows, LANES), jnp.float32),
+            pltpu.VMEM((group, piece_rows, LANES), jnp.float32),
+            pltpu.VMEM((group, piece_rows, LANES), jnp.float32),
             pltpu.VMEM((group - 1, piece_rows, LANES), jnp.float32),
             pltpu.SemaphoreType.DMA((4,)),
             pltpu.SemaphoreType.DMA((2,)),
@@ -297,6 +315,7 @@
             pltpu.SemaphoreType.DMA((n_tm,)),
             pltpu.SemaphoreType.DMA((n_tm,)),
             pltpu.SemaphoreType.DMA((2,)),
+            pltpu.SemaphoreType.DMA((2,)),
         ],
         compiler_params=pltpu.CompilerParams(
             collective_id=0, has_side_effects=True, vmem_limit_bytes=60 * 2**20

time: 20.8 us -> 21 us (level)
  no operation moved by 1% of the time
where the time goes in v3:
time: 21 us; the launch traced here: 20.7 us
  Pallas kernels  19.5 us (93%)
  local copies, waits for them, and re-layouts  1.28 us (6%)
    pallas_call x1, Pallas kernels, body(): pl.pallas_call(functools.partial(kernel, n_tm, n_sub), out_shape=jax.Shap...  19.5 us
    unnamed x1, local copies, waits for them, and re-layouts  1.28 us

profile of v3, /device:TPU:0, one launch (start us, length us, event | category | flops | bytes accessed | tf_op | source)
XLA Modules:
  0.0 20.7 jit_solution(17772853041015806038)
XLA Ops:
  0.0 19.5 %shard_map.46 = f32[8,128]{1,0:T(8,128)} custom-call(s32[1,1,2,2]{3,2,1,0:T(2,128)} %tiles_hbm.1, f32[8,2048]{1,0:T(8,128)} %archive_ref.1, f32[16,127]{1,0:T(8,128)} %tail_hbm.1, f32[16,16]{1,0:T(8,128)} %precision_hbm.1), custom_call_target="tpu_custom_call" | custom-call | tf_op jit(solution)/shard_map/pallas_call | solution.py:294
  19.5 1.3 %copy.6 = f32[1024]{0:T(1024)} copy(f32[1024]{0:T(1024)} %bitcast.1) | data formatting | bytes 8192

commit v4 on v1

--- a/solution.py
+++ b/solution.py
@@ -121,35 +121,34 @@
     whitened = whiten(factor, raw_ref[...])
     for k in range(tiles):
         series_ref[(tm * 2 + ch) * tiles + k] = whitened[:, k * LANES : (k + 1) * LANES]
-    along_time = [None]
-    for back in range(1, n_tm):
-        along_time.append(
+    along_time, to_pair = [None], []
+    for back in range(n_tm):
+        later = lax.rem(tm + back, n_tm)
+        if back:
+            along_time.append(
+                pltpu.make_async_remote_copy(
+                    src_ref=mine,
+                    dst_ref=mine,
+                    send_sem=time_send.at[back],
+                    recv_sem=time_recv.at[back],
+                    device_id={"tm": later},
+                    device_id_type=MESH,
+                )
+            )
+            along_time[back].start()
+        to_pair.append(
             pltpu.make_async_remote_copy(
                 src_ref=mine,
                 dst_ref=mine,
-                send_sem=time_send.at[back],
-                recv_sem=time_recv.at[back],
-                device_id={"tm": lax.rem(tm + back, n_tm)},
+                send_sem=pair_send.at[back],
+                recv_sem=pair_recv.at[back],
+                device_id={"tm": later, "ch": other},
                 device_id_type=MESH,
             )
         )
-        along_time[back].start()
-    to_pair = []
-    for back in range(n_tm):
-        if back:
-            along_time[back].wait_recv()
-        held = chunk(lax.rem(tm + n_tm - back, n_tm), ch)
-        to_pair.append(
-            pltpu.make_async_remote_copy(
-                src_ref=held,
-                dst_ref=held,
-                send_sem=pair_send.at[back],
-                recv_sem=pair_recv.at[back],
-                device_id={"ch": other},
-                device_id_type=MESH,
-            )
-        )
         to_pair[back].start()
+    for copy in along_time[1:]:
+        copy.wait_recv()
     for copy in to_pair:
         copy.wait_recv()
 

time: 20.7 us -> 22.5 us (1.087)
  Pallas kernels: 19.2 us -> 21 us
    pallas_call x1, Pallas kernels: 19.2 us -> 21 us  [body(): pl.pallas_call(functools.partial(kernel, n_tm, n_sub), out_shape=jax.Shap...]
where the time goes in v4:
time: 22.5 us; the launch traced here: 22.3 us
  Pallas kernels  21 us (93%)
  local copies, waits for them, and re-layouts  1.28 us (6%)
    pallas_call x1, Pallas kernels, body(): pl.pallas_call(functools.partial(kernel, n_tm, n_sub), out_shape=jax.Shap...  21 us
    unnamed x1, local copies, waits for them, and re-layouts  1.28 us

profile of v4, /device:TPU:0, one launch (start us, length us, event | category | flops | bytes accessed | tf_op | source)
XLA Modules:
  0.0 22.3 jit_solution(17174884658593625719)
XLA Ops:
  0.0 21.0 %shard_map.46 = f32[8,128]{1,0:T(8,128)} custom-call(s32[1,1,2,2]{3,2,1,0:T(2,128)} %tiles_hbm.1, f32[8,2048]{1,0:T(8,128)} %archive_ref.1, f32[16,127]{1,0:T(8,128)} %tail_hbm.1, f32[16,16]{1,0:T(8,128)} %precision_hbm.1), custom_call_target="tpu_custom_call" | custom-call | tf_op jit(solution)/shard_map/pallas_call | solution.py:272
  21.0 1.3 %copy.6 = f32[1024]{0:T(1024)} copy(f32[1024]{0:T(1024)} %bitcast.1) | data formatting | bytes 8192
